TPU v7x, 512 devices: a whole 4x4x16 slice. The times are simulated.
512 devices in a mesh: ctx: 32 (over x, z_lo, core), tp: 16 (over z_hi, y).
Axes of the slice: x: 4, y: 4, z: 16 (z_hi: 4, z_lo: 4; z = z_hi * 4 + z_lo), core: 2. Of those that a mesh axis runs over, the one named last changes fastest.
Arguments:
- inputs: bfloat16 [3, 8192, 4096], P(None, 'tp', 'ctx'), may hold values from -6 to 6
- short_filters: float32 [3, 3, 8192], P(None, None, 'tp'), may hold values from -3 to 3
- explicit_filter: bfloat16 [512, 128], P('tp'), may hold values from -0.81 to 0.81
- skip_gain: float32 [8192], P('tp'), may hold values from 0.5 to 1.5
- out_weight: bfloat16 [8192, 8192], P('tp', 'ctx'), may hold values from -0.125 to 0.125
- out_cotangent: bfloat16 [8192, 4096], P('tp', 'ctx'), may hold values from -6 to 6
Outputs:
- output: bfloat16 [8192, 4096], P('tp', 'ctx')
- grad_inputs: bfloat16 [3, 8192, 4096], P(None, 'tp', 'ctx')
- grad_filter: float32 [512, 128], P('tp')
- grad_skip: float32 [8192], P('tp')
All inputs are finite; a program needn't handle non-finite values.
Results may differ from a plain program's by a relative error of at most 0.0059.
Values may be sent and summed in bfloat16 or wider, within the bound.
A program may use at most 64 MiB of HBM per device.

v0:
```python
import jax
import jax.numpy as jnp
from jax import lax
from jax.sharding import PartitionSpec as P

GROUP = 16


def toeplitz(filter_rows_in):
    amount = filter_rows_in.shape[0]
    block_len = filter_rows_in.shape[1]
    widened = jnp.concatenate([filter_rows_in, jnp.zeros_like(filter_rows_in)], axis=1)
    tiled = jnp.tile(widened, (1, block_len))
    skewed = tiled[:, : block_len * (2 * block_len - 1)].reshape(
        amount, block_len, 2 * block_len - 1
    )
    current = skewed[:, :, :block_len]
    previous = jnp.concatenate(
        [skewed[:, :, block_len:], jnp.zeros((amount, block_len, 1), filter_rows_in.dtype)], axis=2
    )
    return (current, previous)


def diagonals(matrix):
    amount = matrix.shape[0]
    block_len = matrix.shape[1]
    padded = jnp.pad(matrix, ((0, 0), (0, 0), (0, block_len)))
    flattened = jnp.pad(padded.reshape(amount, 2 * block_len * block_len), ((0, 0), (0, block_len)))
    skewed = flattened.reshape(amount, block_len, 2 * block_len + 1)[:, :, :block_len]
    return jnp.sum(skewed, axis=1)


def short_forward(padded, filters, length):
    summed = filters[:, 0, :, None] * padded[:, :, 2 : 2 + length]
    summed = summed + filters[:, 1, :, None] * padded[:, :, 1 : 1 + length]
    return summed + filters[:, 2, :, None] * padded[:, :, 0:length]


def short_backward(padded, filters, length):
    summed = filters[:, 0, :, None] * padded[:, :, 0:length]
    summed = summed + filters[:, 1, :, None] * padded[:, :, 1 : 1 + length]
    return summed + filters[:, 2, :, None] * padded[:, :, 2 : 2 + length]


def long_forward(extended, current, previous, per_group):
    channels = extended.shape[0]
    block_len = current.shape[1]
    nblocks = extended.shape[1] // block_len - 1
    stacked = extended.reshape(channels // per_group, per_group, nblocks + 1, block_len)
    result = jnp.einsum(
        "gcbs,gst->gcbt", stacked[:, :, 1:], current, preferred_element_type=jnp.float32
    )
    result = result + jnp.einsum(
        "gcbs,gst->gcbt", stacked[:, :, :-1], previous, preferred_element_type=jnp.float32
    )
    return result.reshape(channels, nblocks * block_len)


def long_backward(grad_ext, current, previous, per_group):
    channels = grad_ext.shape[0]
    block_len = current.shape[1]
    nblocks = grad_ext.shape[1] // block_len - 1
    stacked = grad_ext.reshape(channels // per_group, per_group, nblocks + 1, block_len)
    result = jnp.einsum(
        "gcbt,gst->gcbs", stacked[:, :, :-1], current, preferred_element_type=jnp.float32
    )
    result = result + jnp.einsum(
        "gcbt,gst->gcbs", stacked[:, :, 1:], previous, preferred_element_type=jnp.float32
    )
    return result.reshape(channels, nblocks * block_len)


def correlate(extended, grad_resp, per_group, block_len):
    channels = grad_resp.shape[0]
    nblocks = grad_resp.shape[1] // block_len
    ext_blocks = extended.reshape(channels // per_group, per_group, nblocks + 1, block_len)
    grad_blocks = grad_resp.reshape(channels // per_group, per_group, nblocks, block_len)
    corr_now = jnp.einsum(
        "gcbs,gcbt->gst", ext_blocks[:, :, 1:], grad_blocks, preferred_element_type=jnp.float32
    )
    corr_back = jnp.einsum(
        "gcbs,gcbt->gts", ext_blocks[:, :, :-1], grad_blocks, preferred_element_type=jnp.float32
    )
    forward_part = diagonals(corr_now)
    backward_part = diagonals(corr_back)
    shifted = jnp.concatenate(
        [jnp.zeros_like(backward_part[:, :1]), jnp.flip(backward_part[:, 1:], axis=1)], axis=1
    )
    return forward_part + shifted


def project(gated, out_weight, out_cotangent):
    weights = lax.all_gather(out_weight, "ctx", axis=1, tiled=True)
    columns = weights
    summed = lax.psum_scatter(
        lax.dot_general(
            columns, gated, (((0,), (0,)), ((), ())), preferred_element_type=jnp.float32
        ),
        "tp",
        scatter_dimension=0,
        tiled=True,
    )
    columns = weights
    grad_sum = jnp.dot(
        columns,
        lax.all_gather(out_cotangent, "tp", axis=0, tiled=True),
        preferred_element_type=jnp.float32,
    )
    return (summed.astype(jnp.bfloat16), grad_sum.astype(jnp.bfloat16))


def body(inputs, short_filters, explicit_filter, skip_gain, out_weight, out_cotangent):
    block_len = explicit_filter.shape[1]
    channel_view = lax.all_to_all(inputs, "ctx", split_axis=1, concat_axis=2, tiled=True)
    channels = channel_view.shape[1]
    length = channel_view.shape[2]
    first_chan = lax.axis_index("ctx") * channels
    filters = lax.dynamic_slice_in_dim(short_filters, first_chan, channels, 2)
    skip_local = lax.dynamic_slice_in_dim(skip_gain, first_chan, channels, 0)
    per_group = min(channels, GROUP)
    local_groups = channels // per_group
    filter_local = lax.dynamic_slice_in_dim(explicit_filter, first_chan // GROUP, local_groups, 0)
    current, previous = toeplitz(filter_local)
    padded = jnp.pad(channel_view.astype(jnp.float32), ((0, 0), (0, 0), (2, 0)))
    features = short_forward(padded, filters, length)
    query_feat = features[0]
    key_feat = features[1]
    value_feat = features[2]
    product = lax.optimization_barrier((key_feat * value_feat).astype(jnp.bfloat16))
    product_f = product.astype(jnp.float32)
    extended = jnp.concatenate([jnp.zeros((channels, block_len), jnp.bfloat16), product], axis=1)
    response = (
        long_forward(extended, current, previous, per_group) + skip_local[:, None] * product_f
    )
    gated_local = (query_feat * response).astype(jnp.bfloat16)
    gated = lax.all_to_all(gated_local, "ctx", split_axis=1, concat_axis=0, tiled=True)
    output, grad_gated = project(gated, out_weight, out_cotangent)
    grad_local = lax.all_to_all(grad_gated, "ctx", split_axis=0, concat_axis=1, tiled=True)
    grad_full = lax.optimization_barrier(grad_local).astype(jnp.float32)
    grad_query = grad_full * response
    grad_resp = lax.optimization_barrier((grad_full * query_feat).astype(jnp.bfloat16))
    grad_resp_f = grad_resp.astype(jnp.float32)
    grad_ext = jnp.concatenate([grad_resp, jnp.zeros((channels, block_len), jnp.bfloat16)], axis=1)
    grad_prod = (
        long_backward(grad_ext, current, previous, per_group) + skip_local[:, None] * grad_resp_f
    )
    filter_part = correlate(extended, grad_resp, per_group, block_len)
    skip_part = jnp.sum(grad_resp_f * product_f, axis=1)
    filter_all, grad_skip = (
        lax.all_gather(filter_part, "ctx", axis=0, tiled=True),
        lax.all_gather(skip_part, "ctx", axis=0, tiled=True),
    )
    grad_feat = jnp.stack([grad_query, grad_prod * value_feat, grad_prod * key_feat])
    back_pad = jnp.pad(grad_feat, ((0, 0), (0, 0), (0, 2)))
    grad_channel = short_backward(back_pad, filters, length).astype(jnp.bfloat16)
    grad_inputs = lax.all_to_all(grad_channel, "ctx", split_axis=2, concat_axis=1, tiled=True)
    return (output, grad_inputs, filter_all, grad_skip)


def solution(mesh):
    placed = (
        P(None, "tp", "ctx"),
        P(None, None, "tp"),
        P("tp", None),
        P("tp"),
        P("tp", "ctx"),
        P("tp", "ctx"),
    )
    return jax.shard_map(
        body,
        mesh=mesh,
        in_specs=placed,
        out_specs=(P("tp", "ctx"), P(None, "tp", "ctx"), P("tp", None), P("tp")),
        check_vma=False,
    )
```

profile of v0, /device:TPU:1, one launch (start us, length us, event | category | flops | bytes accessed | tf_op | source)
XLA Modules:
  0.0 410.5 jit_solution(8315195538780197668)
XLA Ops:
  7.2 0.7 all-gather.6.cloned.1.call-update
  8.0 0.7 all-gather.4.cloned.1.call-update
  8.7 2.2 copy.91
  10.8 10.4 %all-to-all-start = ((bf16[3,512,128]{2,0,1:T(4,128)(2,1)}), bf16[3,512,128]{2,0,1:T(4,128)(2,1)S(1)}, u32[]{:S(2)}, u32[]{:S(2)}) async-start(bf16[3,512,128]{2,0,1:T(4,128)(2,1)} %copy.91), calls=%async_computation | async-start | bytes 1048576 | tf_op jit(solution)/shard_map/all_to_all | solution.py:114
  21.3 0.8 dynamic_slice.11
  22.0 0.9 constant_dynamic-slice_fusion.1
  23.1 0.4 slice_reduce_fusion
  23.8 14.4 %all-to-all-done = bf16[3,512,128]{2,0,1:T(4,128)(2,1)S(1)} async-done(((bf16[3,512,128]{2,0,1:T(4,128)(2,1)}), bf16[3,512,128]{2,0,1:T(4,128)(2,1)S(1)}, u32[]{:S(2)}, u32[]{:S(2)}) %all-to-all-start) | async-done | bytes 393248 | tf_op jit(solution)/shard_map/all_to_all | solution.py:114
  38.6 72.1 %all-gather.6.cloned.1.call-done = bf16[8192,128]{1,0:T(8,128)(2,1)} async-done(((bf16[512,128]{1,0:T(8,128)(2,1)}), bf16[8192,128]{1,0:T(8,128)(2,1)}) %all-gather.6.cloned.1.call-update) | async-done | bytes 2097168 | tf_op jit(solution)/shard_map/all_gather | solution.py:106
  110.7 91.0 %all-gather.4.cloned.1.call-done = bf16[512,8192]{1,0:T(8,128)(2,1)} async-done(((bf16[512,256]{1,0:T(8,128)(2,1)}), bf16[512,8192]{1,0:T(8,128)(2,1)}) %all-gather.4.cloned.1.call-update) | async-done | bytes 8388624 | tf_op jit(solution)/shard_map/all_gather | solution.py:93
  201.7 7.0 %convolution_convert_fusion = bf16[512,128]{1,0:T(8,128)(2,1)} fusion(bf16[512,8192]{1,0:T(8,128)(2,1)} %all-gather.4.cloned.1.call-done, bf16[8192,128]{1,0:T(8,128)(2,1)} %all-gather.6.cloned.1.call-done), kind=kOutput, calls=%fused_computation.3 | convolution fusion | flops 1073807360 | bytes 10616832 | tf_op jit(solution)/shard_map/dot_general | solution.py:104
  208.7 4.7 %all-to-all-start.2 = ((bf16[32,16,128]{2,1,0:T(8,128)(2,1)}), bf16[32,16,128]{2,1,0:T(8,128)(2,1)S(1)}, u32[]{:S(2)}, u32[]{:S(2)}) async-start(bf16[32,16,128]{2,1,0:T(8,128)(2,1)} %bitcast.14), calls=%async_computation.3 | async-start | bytes 262144 | tf_op jit(solution)/shard_map/all_to_all | solution.py:138
  213.4 0.5 multiply_add_fusion
  213.9 8.2 %all-to-all-done.2 = bf16[32,16,128]{2,1,0:T(8,128)(2,1)S(1)} async-done(((bf16[32,16,128]{2,1,0:T(8,128)(2,1)}), bf16[32,16,128]{2,1,0:T(8,128)(2,1)S(1)}, u32[]{:S(2)}, u32[]{:S(2)}) %all-to-all-start.2) | async-done | bytes 131104 | tf_op jit(solution)/shard_map/all_to_all | solution.py:138
  223.1 0.5 multiply_bitcast_fusion.1
  223.6 12.1 %all_to_all.65 = bf16[16,32,128]{2,0,1:T(8,128)(2,1)S(1)} all-to-all(bf16[16,32,128]{2,0,1:T(8,128)(2,1)S(1)} %bitcast.143), channel_id=1, replica_groups=mesh['ctx'=32,'tp'=16] {'ctx'}, dimensions={1} | all-to-all | bytes 262144 | tf_op jit(solution)/shard_map/all_to_all | solution.py:136
  235.7 6.7 %convolution_bitcast_fusion = f32[8192,128]{0,1:T(8,128)} fusion(bf16[512,128]{1,0:T(8,128)(2,1)S(1)} %bitcast.142, bf16[512,8192]{1,0:T(8,128)(2,1)} %all-gather.4.cloned.1.call-done), kind=kOutput, calls=%fused_computation | convolution fusion | flops 1073741824 | bytes 12713984 | tf_op jit(solution)/shard_map/dot_general | solution.py:96
  242.4 0.5 add_convert_fusion
  242.9 4.6 %copy.95 = bf16[3,16,4096]{1,0,2:T(4,128)(2,1)} copy(bf16[3,16,4096]{2,1,0:T(8,128)(2,1)S(1)} %add_convert_fusion) | data formatting | bytes 786432 | tf_op jit(solution)/shard_map/convert_element_type | solution.py:155
  247.6 7.5 %reshape.162 = bf16[32,2,3072]{2,1,0:T(2,128)(2,1)} reshape(bf16[4096,3,16]{2,1,0:T(4,128)(2,1)} %bitcast.135) | data formatting | bytes 786432
  255.0 3.9 all-to-all-start.3
  259.0 1.3 dynamic-slice
  261.3 0.3 pad_reduce_fusion.1
  261.7 0.3 reshape.142
  262.4 0.3 pad_reduce_fusion
  263.4 55.6 %all-gather = f32[32,1,128]{2,1,0:T(1,128)S(1)} all-gather(f32[1,1,128]{2,1,0:T(1,128)S(1)} %fusion.12), channel_id=1, replica_groups=mesh['ctx'=32,'tp'=16] {'ctx'}, dimensions={0}, use_global_device_ids=true | all-gather | bytes 16896 | tf_op jit(solution)/shard_map/all_gather | solution.py:150
  319.2 70.8 %all-reduce.10 = f32[512]{0:T(512)} all-reduce(f32[512]{0:T(512)S(1)} %dynamic-update-slice), channel_id=1, replica_groups=mesh['ctx'=32,'tp'=16] {'ctx'}, use_global_device_ids=true, to_apply=%add.10 | all-reduce | flops 512 | bytes 4096
  390.0 5.6 %reshape.163 = bf16[4096,3,16]{2,1,0:T(4,128)(2,1)} reshape(bf16[32,2,3072]{2,1,0:T(2,128)(2,1)S(1)} %all-to-all-done.3) | data formatting | bytes 786432
  395.7 6.0 %copy.96 = bf16[3,32,16,128]{3,2,1,0:T(8,128)(2,1)} copy(bf16[3,32,16,128]{2,0,3,1:T(4,128)(2,1)} %bitcast.136) | data formatting | bytes 786432 | tf_op jit(solution)/shard_map/all_to_all | solution.py:156
  401.7 1.0 convert_element_type.56
  402.6 0.8 copy.97
  403.4 0.6 copy.132
  (45 shorter events, 3.7 us)
Async XLA Ops:
  7.2 15.7 %copy-start = (bf16[32,128]{1,0:T(8,128)(2,1)S(1)}, bf16[32,128]{1,0:T(8,128)(2,1)}, u32[]{:S(2)}) copy-start(bf16[32,128]{1,0:T(8,128)(2,1)} %param.8) | copy-start | bytes 24580
  7.2 103.5 %all-gather.6.cloned.1.call-start = ((), (), s32[]{:S(2)}) async-start(), calls=%async_computation.7 | async-start | bytes 2228224 | tf_op jit(solution)/shard_map/all_gather | solution.py:106
  7.9 193.8 %all-gather.4.cloned.1.call-start = ((), (), s32[]{:S(2)}) async-start(), calls=%async_computation.5 | async-start | bytes 8650752 | tf_op jit(solution)/shard_map/all_gather | solution.py:93
  10.8 27.3 %all-to-all-start = ((bf16[3,512,128]{2,0,1:T(4,128)(2,1)}), bf16[3,512,128]{2,0,1:T(4,128)(2,1)S(1)}, u32[]{:S(2)}, u32[]{:S(2)}) async-start(bf16[3,512,128]{2,0,1:T(4,128)(2,1)} %copy.91), calls=%async_computation | async-start | bytes 1048576 | tf_op jit(solution)/shard_map/all_to_all | solution.py:114
  208.7 13.4 %all-to-all-start.2 = ((bf16[32,16,128]{2,1,0:T(8,128)(2,1)}), bf16[32,16,128]{2,1,0:T(8,128)(2,1)S(1)}, u32[]{:S(2)}, u32[]{:S(2)}) async-start(bf16[32,16,128]{2,1,0:T(8,128)(2,1)} %bitcast.14), calls=%async_computation.3 | async-start | bytes 262144 | tf_op jit(solution)/shard_map/all_to_all | solution.py:138
  213.4 188.3 %reduce-scatter.2.cloned.1.call-start = ((), (), s32[]{:S(2)}) async-start(), calls=%async_computation.6 | async-start | bytes 4456448 | tf_op jit(solution)/shard_map/reduce_scatter | solution.py:95
  255.0 135.0 %all-to-all-start.3 = ((bf16[32,2,3072]{2,1,0:T(2,128)(2,1)}), bf16[32,2,3072]{2,1,0:T(2,128)(2,1)S(1)}, u32[]{:S(2)}, u32[]{:S(2)}) async-start(bf16[32,2,3072]{2,1,0:T(2,128)(2,1)} %reshape.162), calls=%async_computation.4 | async-start | bytes 786432 | tf_op jit(solution)/shard_map/all_to_all | solution.py:156
Sparse Core Ops, SparseCore 0:
  11.0 99.6 all-gather.5
  112.8 88.8 all-gather.3
  242.5 155.1 reduce-scatter.1
where the time goes:
time: 418 us; the launch traced here: 411 us
  waiting for transfers between devices  187 us (45%)
  blocking collectives  139 us (33%)
  local copies, waits for them, and re-layouts  33.7 us (8%)
  starting transfers between devices  19.1 us (5%)
  matrix products  14.8 us (4%)
  between operations  14.7 us (4%)
    all_gather x1, waiting for transfers between devices, project(): weights = lax.all_gather(out_weight, 'ctx', axis=1, tiled=True)  91 us
    all_gather x1, waiting for transfers between devices, project(): lax.all_gather(out_cotangent, 'tp', axis=0, tiled=True)  72.1 us
    unnamed x1, blocking collectives  70.8 us
    all_gather x1, blocking collectives, body(): lax.all_gather(filter_part, 'ctx', axis=0, tiled=True)  55.6 us
    unnamed x19, local copies, waits for them, and re-layouts  18.5 us
    all_to_all x1, waiting for transfers between devices, body(): lax.all_to_all(inputs, 'ctx', split_axis=1, concat_axis=2, tiled=True)  14.4 us
    all_to_all x1, blocking collectives, body(): lax.all_to_all(gated_local, 'ctx', split_axis=1, concat_axis=0, tiled=True)  12.1 us
    all_to_all x1, starting transfers between devices, body(): lax.all_to_all(inputs, 'ctx', split_axis=1, concat_axis=2, tiled=True)  10.4 us
  transfers between devices with their start and end apart: 6, of which 4 were waited for; matrix products, arithmetic and copies ran while one was open for 8% of the time, Pallas kernels for 0%

commit v1 on v0

v1 whole, which is shorter than its diff:
```python
import jax
import jax.numpy as jnp
from jax import lax
from jax.experimental import pallas as pl
from jax.experimental.pallas import tpu as pltpu
from jax.sharding import PartitionSpec as P

MESH = pl.DeviceIdType.MESH
BF = jnp.bfloat16
F32 = jnp.float32
N_SEND = 128
N_RECV = 128


def nt_dot(a, b):
    return lax.dot_general(a, b, (((1,), (1,)), ((), ())), preferred_element_type=F32)


def tn_dot(a, b):
    return lax.dot_general(a, b, (((0,), (0,)), ((), ())), preferred_element_type=F32)


def nn_dot(a, b):
    return jnp.dot(a, b, preferred_element_type=F32)


def kernel(
    inp, taps, filt, skip, w_hbm, cot_hbm,
    out, ginp, gfilt, gskip,
    wall, call, toep, coef, tail_out, tail_in, tail_cols, qf, kf, vf, prod, prev, resp, gated_t,
    acc, part, gout, gnext, gprod, gtail_out, gtail_in, gtail_cols,
    y_half, y_full, y_stage, z_half, z_full, z_stage, z_own,
    pay, pay_in, local_sem, ssem, rsem, wz_sem, wsib_sem,
):
    ctx, tp = lax.axis_index("ctx"), lax.axis_index("tp")
    x, zl, core = ctx // 8, (ctx // 2) % 4, ctx % 2
    zh, y = tp // 4, tp % 4

    def at_ctx(x_, zl_, core_):
        return ((x_ * 4 + zl_) * 2 + core_, tp)

    def at_tp(zh_, y_):
        return (ctx, zh_ * 4 + y_)

    def plus(v, d):
        return (v + d) % 4

    x_right, x_left, x_far = at_ctx(plus(x, 1), zl, core), at_ctx(plus(x, 3), zl, core), at_ctx(plus(x, 2), zl, core)
    l_up, l_down, l_far = at_ctx(x, plus(zl, 1), core), at_ctx(x, plus(zl, 3), core), at_ctx(x, plus(zl, 2), core)
    sibling = at_ctx(x, zl, 1 - core)
    later, earlier = ((ctx + 1) % 32, tp), ((ctx + 31) % 32, tp)
    h_right, h_left = at_tp(plus(zh, 1), y), at_tp(plus(zh, 3), y)
    y_right, y_left = at_tp(zh, plus(y, 1)), at_tp(zh, plus(y, 3))

    upper = zl // 2
    inner = zl + upper * (3 - 2 * zl)
    step_dir = 1 - 2 * upper
    z_in = at_ctx(x, zl + step_dir, core)
    z_out = at_ctx(x, (zl - step_dir + 4) % 4, core)

    def unmirror(v):
        return v + upper * (3 - 2 * v)

    line = [zl, unmirror(1 - inner), unmirror(2), unmirror(3)]

    own = x * 4 + zl
    copy_w = pltpu.make_async_copy(w_hbm, wall.at[own, core], local_sem.at[0])
    copy_c = pltpu.make_async_copy(cot_hbm, call.at[tp], local_sem.at[1])
    copy_w.start()
    copy_c.start()

    partners = [x_right, x_left, x_far, l_up, l_down, l_far, sibling, later, earlier, h_right, h_left, y_right, y_left]
    barrier = pltpu.get_barrier_semaphore()
    for who in partners:
        pl.semaphore_signal(barrier, inc=1, device_id=who, device_id_type=MESH)

    count = {"s": 0, "r": 0}
    sends = []

    def new_recv():
        count["r"] += 1
        return rsem.at[count["r"] - 1]

    def send(src, dst, sem, who, when=None):
        copy = pltpu.make_async_remote_copy(src, dst, ssem.at[count["s"]], sem, device_id=who, device_id_type=MESH)
        count["s"] += 1
        if when is None:
            copy.start()
        else:
            pl.when(when)(lambda: copy.start())
        sends.append((copy, when))

    def arrived(dst, sem):
        pltpu.make_async_remote_copy(dst, dst, ssem.at[0], sem, device_id=sibling, device_id_type=MESH).wait_recv()

    for a in range(3):
        turned = inp[a].astype(F32).T
        tail_out[2 * a:2 * a + 2, :] = turned[126:128, :]
    tail_out[6:8, :] = jnp.zeros((2, 512), F32)

    copy_w.wait()
    copy_c.wait()
    pl.semaphore_wait(barrier, len(partners))

    r_tail = new_recv()
    send(tail_out, tail_in, r_tail, later)

    x_sems = [[new_recv() for _ in range(4)] for _ in range(4)]

    def w_start(s):
        n = x * 4 + line[s]
        if s > 0:
            arrived(wall.at[n, core], wz_sem.at[line[s]])
        block = wall.at[n, core]
        if s == 0:
            send(block, block, wz_sem.at[line[s]], z_in)
            send(block, block, wz_sem.at[line[s]], z_out, inner == 1)
        elif s == 1:
            send(block, block, wz_sem.at[line[s]], z_in, inner == 1)
        else:
            send(block, block, wz_sem.at[line[s]], z_out, inner == 1)
        send(block, block, x_sems[s][0], x_right)
        send(block, block, x_sems[s][1], x_left)
        send(block, block, wsib_sem.at[4 * s], sibling)

    def w_near(s):
        n = plus(x, 3) * 4 + line[s]
        block = wall.at[n, core]
        arrived(block, x_sems[s][0])
        half = wall.at[n, core, pl.ds(0, 256), :]
        send(half, half, x_sems[s][2], x_right)
        send(block, block, wsib_sem.at[4 * s + 1], sibling)
        n = plus(x, 1) * 4 + line[s]
        block = wall.at[n, core]
        arrived(block, x_sems[s][1])
        half = wall.at[n, core, pl.ds(256, 256), :]
        send(half, half, x_sems[s][3], x_left)
        send(block, block, wsib_sem.at[4 * s + 2], sibling)

    def w_far(s):
        n = plus(x, 2) * 4 + line[s]
        arrived(wall.at[n, core, pl.ds(0, 256), :], x_sems[s][2])
        arrived(wall.at[n, core, pl.ds(256, 256), :], x_sems[s][3])
        block = wall.at[n, core]
        send(block, block, wsib_sem.at[4 * s + 3], sibling)

    def w_sibling(s):
        for i, d in enumerate((0, 3, 1, 2)):
            n = plus(x, d) * 4 + line[s]
            arrived(wall.at[n, 1 - core], wsib_sem.at[4 * s + i])

    c_zsems = [new_recv() for _ in range(4)]
    c_ysems = [[new_recv() for _ in range(4)] for _ in range(4)]
    lo, hi = pl.ds(0, 256), pl.ds(256, 256)

    def c_start():
        block = call.at[tp]
        send(block, block, c_zsems[0], h_right)
        send(block, block, c_zsems[1], h_left)
        c_ysend(0)

    def c_ysend(d):
        block = call.at[plus(zh, d) * 4 + y]
        send(block, block, c_ysems[d][0], y_right)
        send(block, block, c_ysems[d][1], y_left)

    def c_znear():
        n = plus(zh, 3) * 4 + y
        arrived(call.at[n], c_zsems[0])
        half = call.at[n, lo, :]
        send(half, half, c_zsems[2], h_right)
        n = plus(zh, 1) * 4 + y
        arrived(call.at[n], c_zsems[1])
        half = call.at[n, hi, :]
        send(half, half, c_zsems[3], h_left)
        c_ysend(3)
        c_ysend(1)

    def c_zfar():
        n = plus(zh, 2) * 4 + y
        arrived(call.at[n, lo, :], c_zsems[2])
        arrived(call.at[n, hi, :], c_zsems[3])
        c_ysend(2)

    def c_ynear(d):
        n = plus(zh, d) * 4 + plus(y, 3)
        arrived(call.at[n], c_ysems[d][0])
        half = call.at[n, lo, :]
        send(half, half, c_ysems[d][2], y_right)
        n = plus(zh, d) * 4 + plus(y, 1)
        arrived(call.at[n], c_ysems[d][1])
        half = call.at[n, hi, :]
        send(half, half, c_ysems[d][3], y_left)

    def c_yfar(d):
        n = plus(zh, d) * 4 + plus(y, 2)
        arrived(call.at[n, lo, :], c_ysems[d][2])
        arrived(call.at[n, hi, :], c_ysems[d][3])

    w_start(0)
    c_start()

    table = jnp.concatenate([taps[0], taps[1], taps[2], skip[...], jnp.zeros((6, 512), F32)], axis=0)
    coef[...] = table.T

    def build(g8, carry):
        rows8 = filt[pl.ds(pl.multiple_of(g8 * 16, 16), 16), :].astype(F32)
        for r in range(16):
            row = jnp.concatenate([rows8[r:r + 1, :], jnp.zeros((1, 128), F32)], axis=1)
            wide = jnp.broadcast_to(row, (128, 256))
            toep[g8 * 16 + r] = pltpu.roll(wide, 0, 1, stride=1, stride_axis=0).astype(BF)
        return carry

    lax.fori_loop(0, 2, build, 0)

    arrived(tail_in, r_tail)
    tail_cols[...] = jnp.where(ctx == 0, 0.0, tail_in[...]).T

    lane = lax.broadcasted_iota(jnp.int32, (64, 128), 1)

    def featurize(i, carry):
        rows = pl.ds(pl.multiple_of(i * 64, 64), 64)
        co = coef[rows, :]
        tl = tail_cols[rows, :]
        feats = []
        for a in range(3):
            v = inp[a, rows, :].astype(F32)
            t126, t127 = tl[:, 2 * a:2 * a + 1], tl[:, 2 * a + 1:2 * a + 2]
            v1 = jnp.where(lane == 0, t127, pltpu.roll(v, 1, 1))
            v2 = jnp.where(lane == 0, t126, jnp.where(lane == 1, t127, pltpu.roll(v, 2, 1)))
            feats.append(co[:, 3 * a:3 * a + 1] * v + co[:, 3 * a + 1:3 * a + 2] * v1 + co[:, 3 * a + 2:3 * a + 3] * v2)
        qf[rows, :] = feats[0]
        kf[rows, :] = feats[1]
        vf[rows, :] = feats[2]
        prod[rows, :] = (feats[1] * feats[2]).astype(BF)
        return carry

    lax.fori_loop(0, 8, featurize, 0)
    r_prod = new_recv()
    send(prod, prev, r_prod, later)

    w_start(1)
    w_near(0)

    arrived(prev, r_prod)

    @pl.when(ctx == 0)
    def _():
        prev[...] = jnp.zeros((512, 128), BF)

    def convolve(i, carry):
        pieces = []
        for j in range(8):
            rows = pl.ds(pl.multiple_of(i * 128 + j * 16, 16), 16)
            g = i * 8 + j
            cur = prod[rows, :]
            r = nn_dot(cur, toep[g, :, 0:128]) + nn_dot(prev[rows, :], toep[g, :, 128:256])
            r = r + coef[rows, 9:10] * cur.astype(F32)
            resp[rows, :] = r
            pieces.append(qf[rows, :] * r)
        gated_t[:, pl.ds(pl.multiple_of(i * 128, 128), 128)] = jnp.concatenate(pieces, axis=0).T.astype(BF)
        return carry

    lax.fori_loop(0, 2, convolve, 0)
    w_start(2)
    w_far(0)
    c_ynear(0)
    lax.fori_loop(2, 4, convolve, 0)
    w_near(1)
    c_znear()

    acc[...] = jnp.zeros((512, 128), F32)

    def forward(s):
        def one(i, carry):
            n = plus(x, i) * 4 + line[s]
            for k in range(2):
                part[n, :, 256 * k:256 * (k + 1)] = nn_dot(gated_t[...], wall[n, k]).astype(BF)
            return carry

        lax.fori_loop(0, 4, one, 0)

    def backward(s):
        def one(r, carry):
            rows = pl.ds(pl.multiple_of(r * 128, 128), 128)
            total = acc[rows, :]
            for d in range(4):
                n = plus(x, d) * 4 + line[s]
                for k in range(2):
                    total = total + nn_dot(wall[n, k, rows, :], call[n, 256 * k:256 * (k + 1), :])
            acc[rows, :] = total
            return carry

        lax.fori_loop(0, 4, one, 0)

    w_sibling(0)
    forward(0)
    w_start(3)
    w_far(1)
    c_zfar()
    c_yfar(0)
    c_ynear(3)
    c_ynear(1)
    w_near(2)
    w_sibling(1)
    forward(1)
    c_ynear(2)
    c_yfar(3)
    c_yfar(1)
    w_far(2)
    c_yfar(2)
    w_sibling(2)
    forward(2)
    backward(0)
    w_near(3)
    backward(1)
    backward(2)
    w_far(3)
    w_sibling(3)
    forward(3)

    yh = [[new_recv() for _ in range(2)] for _ in range(4)]
    yf = [[new_recv() for _ in range(2)] for _ in range(4)]
    order = [2, 1, 3, 0]
    top, low = pl.ds(0, 64), pl.ds(64, 64)
    for d in order:
        far = plus(zh, d) * 4 + plus(y, 2)
        send(part.at[far, top, :], y_half.at[d, 0], yh[d][0], y_right)
        send(part.at[far, low, :], y_half.at[d, 1], yh[d][1], y_left)
    backward(3)

    def at_response(i, carry):
        rows = pl.ds(pl.multiple_of(i * 64, 64), 64)
        gg = acc[rows, :].astype(BF).astype(F32)
        gout[rows, :] = (gg * qf[rows, :]).astype(BF)
        qf[rows, :] = gg * resp[rows, :]
        return carry

    lax.fori_loop(0, 8, at_response, 0)
    r_gout = new_recv()
    send(gout, gnext, r_gout, earlier)

    for d in order:
        group = plus(zh, d) * 4
        arrived(y_half.at[d, 0], yh[d][0])
        n = group + plus(y, 1)
        y_stage[d, 0, 0:64, :] = (part[n, 0:64, :].astype(F32) + y_half[d, 0].astype(F32)).astype(BF)
        y_stage[d, 0, 64:128, :] = part[n, 64:128, :]
        send(y_stage.at[d, 0], y_full.at[d, 0], yf[d][0], y_right)
        arrived(y_half.at[d, 1], yh[d][1])
        n = group + plus(y, 3)
        y_stage[d, 1, 0:64, :] = part[n, 0:64, :]
        y_stage[d, 1, 64:128, :] = (part[n, 64:128, :].astype(F32) + y_half[d, 1].astype(F32)).astype(BF)
        send(y_stage.at[d, 1], y_full.at[d, 1], yf[d][1], y_left)

    arrived(gnext, r_gout)

    @pl.when(ctx == 31)
    def _():
        gnext[...] = jnp.zeros((512, 128), BF)

    def y_sum(d):
        arrived(y_full.at[d, 0], yf[d][0])
        arrived(y_full.at[d, 1], yf[d][1])
        mine = part[plus(zh, d) * 4 + y].astype(F32)
        return mine + y_full[d, 0].astype(F32) + y_full[d, 1].astype(F32)

    zhs = [new_recv() for _ in range(2)]
    zfs = [new_recv() for _ in range(2)]

    def grad_product(i, carry):
        for j in range(8):
            rows = pl.ds(pl.multiple_of(i * 128 + j * 16, 16), 16)
            g = i * 8 + j
            gr = gout[rows, :]
            r = nt_dot(gr, toep[g, :, 0:128]) + nt_dot(gnext[rows, :], toep[g, :, 128:256])
            r = r + coef[rows, 9:10] * gr.astype(F32)
            k = kf[rows, :]
            kf[rows, :] = r * vf[rows, :]
            vf[rows, :] = r * k
        return carry

    lax.fori_loop(0, 4, grad_product, 0)
    for a, ref in enumerate((qf, kf, vf)):
        gtail_out[2 * a:2 * a + 2, :] = ref[:, 0:128].T[0:2, :]
    gtail_out[6:8, :] = jnp.zeros((2, 512), F32)
    r_gtail = new_recv()
    send(gtail_out, gtail_in, r_gtail, earlier)

    z_stage[2] = y_sum(2).astype(BF)
    send(z_stage.at[2, top, :], z_half.at[0], zhs[0], h_right)
    send(z_stage.at[2, low, :], z_half.at[1], zhs[1], h_left)

    turn = (
        lax.broadcasted_iota(jnp.int32, (128, 128), 0) + lax.broadcasted_iota(jnp.int32, (128, 128), 1) == 127
    ).astype(F32).astype(BF)

    def correlate(i, carry):
        base = pl.multiple_of(i * 128, 128)
        cur = nn_dot(prod[pl.ds(base, 128), :], turn).astype(BF)
        back = nn_dot(prev[pl.ds(base, 128), :], turn).astype(BF)
        sums = []
        for j in range(8):
            gr = gout[pl.ds(pl.multiple_of(i * 128 + j * 16, 16), 16), :]
            one = tn_dot(cur[16 * j:16 * (j + 1), :], gr)
            two = tn_dot(back[16 * j:16 * (j + 1), :], gr)
            both = pltpu.roll(jnp.concatenate([one, two], axis=1), 129, 1, stride=1, stride_axis=0)
            sums.append(jnp.sum(both[:, 0:128], axis=0, keepdims=True))
        pay[0, pl.ds(pl.multiple_of(i * 8, 8), 8), :] = jnp.concatenate(sums, axis=0)
        return carry

    lax.fori_loop(0, 4, correlate, 0)
    for i in range(4):
        both = gout[128 * i:128 * (i + 1), :].astype(F32) * prod[128 * i:128 * (i + 1), :].astype(F32)
        pay[0, 32 + i:33 + i, :] = jnp.sum(both.T, axis=0, keepdims=True)
    pay[0, 36:40, :] = jnp.zeros((4, 128), F32)

    def exchange(stage, targets):
        sems = [new_recv() for _ in targets]
        for i, who in enumerate(targets):
            send(pay.at[stage], pay_in.at[stage, i], sems[i], who)
        return sems

    def collect(stage, sems):
        total = pay[stage]
        for i, sem in enumerate(sems):
            arrived(pay_in.at[stage, i], sem)
            total = total + pay_in[stage, i]
        return total

    px = exchange(0, [x_right, x_left, x_far])

    for d, way, who in ((1, 0, h_right), (3, 1, h_left)):
        s = y_sum(d)
        arrived(z_half.at[way], zhs[way])
        half = z_half[way].astype(F32)
        if way == 0:
            z_stage[d, 0:64, :] = (s[0:64, :] + half).astype(BF)
            z_stage[d, 64:128, :] = s[64:128, :].astype(BF)
        else:
            z_stage[d, 0:64, :] = s[0:64, :].astype(BF)
            z_stage[d, 64:128, :] = (s[64:128, :] + half).astype(BF)
        send(z_stage.at[d], z_full.at[way], zfs[way], who)

    z_own[...] = y_sum(0)
    pay[1] = collect(0, px)
    pz = exchange(1, [l_up, l_down, l_far])

    arrived(gtail_in, r_gtail)
    gtail_cols[...] = jnp.where(ctx == 31, 0.0, gtail_in[...]).T

    def short_back(i, carry):
        rows = pl.ds(pl.multiple_of(i * 64, 64), 64)
        co = coef[rows, :]
        tl = gtail_cols[rows, :]
        for a, ref in enumerate((qf, kf, vf)):
            v = ref[rows, :]
            t0, t1 = tl[:, 2 * a:2 * a + 1], tl[:, 2 * a + 1:2 * a + 2]
            v1 = jnp.where(lane == 127, t0, pltpu.roll(v, 127, 1))
            v2 = jnp.where(lane == 126, t0, jnp.where(lane == 127, t1, pltpu.roll(v, 126, 1)))
            r = co[:, 3 * a:3 * a + 1] * v + co[:, 3 * a + 1:3 * a + 2] * v1 + co[:, 3 * a + 2:3 * a + 3] * v2
            ginp[a, rows, :] = r.astype(BF)
        return carry

    lax.fori_loop(0, 8, short_back, 0)
    pay[2] = collect(1, pz)
    pc = exchange(2, [sibling])
    total = collect(2, pc)
    gfilt[...] = total[0:32, :]
    gskip[...] = total[32:40, :]

    arrived(z_full.at[0], zfs[0])
    arrived(z_full.at[1], zfs[1])
    final = z_own[...] + z_full[0].astype(F32) + z_full[1].astype(F32)
    out[...] = final.T.astype(BF)

    for copy, when in sends:
        if when is None:
            copy.wait_send()
        else:
            pl.when(when)(lambda copy=copy: copy.wait_send())
    assert count["s"] <= N_SEND and count["r"] <= N_RECV


def body(inputs, short_filters, explicit_filter, skip_gain, out_weight, out_cotangent):
    vmem = pl.BlockSpec(memory_space=pltpu.VMEM)
    hbm = pl.BlockSpec(memory_space=pl.ANY)
    out, ginp, gfilt, gskip = pl.pallas_call(
        kernel,
        out_shape=(
            jax.ShapeDtypeStruct((512, 128), BF),
            jax.ShapeDtypeStruct((3, 512, 128), BF),
            jax.ShapeDtypeStruct((32, 128), F32),
            jax.ShapeDtypeStruct((8, 128), F32),
        ),
        in_specs=[vmem, vmem, vmem, vmem, hbm, hbm],
        out_specs=(vmem, vmem, vmem, vmem),
        scratch_shapes=[
            pltpu.VMEM((16, 2, 512, 256), BF),
            pltpu.VMEM((16, 512, 128), BF),
            pltpu.VMEM((32, 128, 256), BF),
            pltpu.VMEM((512, 16), F32),
            pltpu.VMEM((8, 512), F32),
            pltpu.VMEM((8, 512), F32),
            pltpu.VMEM((512, 8), F32),
            pltpu.VMEM((512, 128), F32),
            pltpu.VMEM((512, 128), F32),
            pltpu.VMEM((512, 128), F32),
            pltpu.VMEM((512, 128), BF),
            pltpu.VMEM((512, 128), BF),
            pltpu.VMEM((512, 128), F32),
            pltpu.VMEM((128, 512), BF),
            pltpu.VMEM((512, 128), F32),
            pltpu.VMEM((16, 128, 512), BF),
            pltpu.VMEM((512, 128), BF),
            pltpu.VMEM((512, 128), BF),
            pltpu.VMEM((8, 128), F32),
            pltpu.VMEM((8, 512), F32),
            pltpu.VMEM((8, 512), F32),
            pltpu.VMEM((512, 8), F32),
            pltpu.VMEM((4, 2, 64, 512), BF),
            pltpu.VMEM((4, 2, 128, 512), BF),
            pltpu.VMEM((4, 2, 128, 512), BF),
            pltpu.VMEM((2, 64, 512), BF),
            pltpu.VMEM((2, 128, 512), BF),
            pltpu.VMEM((4, 128, 512), BF),
            pltpu.VMEM((128, 512), F32),
            pltpu.VMEM((3, 40, 128), F32),
            pltpu.VMEM((3, 3, 40, 128), F32),
            pltpu.SemaphoreType.DMA((2,)),
            pltpu.SemaphoreType.DMA((N_SEND,)),
            pltpu.SemaphoreType.DMA((N_RECV,)),
            pltpu.SemaphoreType.DMA((4,)),
            pltpu.SemaphoreType.DMA((16,)),
        ],
        compiler_params=pltpu.CompilerParams(
            collective_id=0, has_side_effects=True, vmem_limit_bytes=48 * 1024 * 1024
        ),
        cost_estimate=pl.CostEstimate(flops=2600000000, bytes_accessed=4000000, transcendentals=0),
    )(inputs, short_filters, explicit_filter, skip_gain.reshape(1, 512), out_weight, out_cotangent)
    return (out, ginp, gfilt, gskip[0:4].reshape(512))


def solution(mesh):
    placed = (
        P(None, "tp", "ctx"),
        P(None, None, "tp"),
        P("tp", None),
        P("tp"),
        P("tp", "ctx"),
        P("tp", "ctx"),
    )
    return jax.shard_map(
        body,
        mesh=mesh,
        in_specs=placed,
        out_specs=(P("tp", "ctx"), P(None, "tp", "ctx"), P("tp", None), P("tp")),
        check_vma=False,
    )
```

time: 418 us -> 115 us (0.28); the launches traced: 411 us -> 115 us
  waiting for transfers between devices: 187 us -> 0 us
  blocking collectives: 139 us -> 0 us
  Pallas kernels: 0 us -> 107 us
  local copies, waits for them, and re-layouts: 33.7 us -> 7.54 us
  starting transfers between devices: 19.1 us -> 0 us
  matrix products: 14.8 us -> 0 us
  between operations: 14.7 us -> 0.66 us
    all_gather x2 -> x0, waiting for transfers between devices: 163 us -> none  [the longest x1 91 us: project(): weights = lax.all_gather(out_weight, 'ctx', axis=1, tiled=True)]
    pallas_call x0 -> x1, Pallas kernels: none -> 107 us  [body(): pl.pallas_call(kernel, out_shape=(jax.ShapeDtypeStruct((512, 128), BF), j...]
    unnamed x1 -> x0, blocking collectives: 70.8 us -> none
    all_gather x1 -> x0, blocking collectives: 55.6 us -> none  [body(): lax.all_gather(filter_part, 'ctx', axis=0, tiled=True)]
    all_to_all x3 -> x0, waiting for transfers between devices: 22.6 us -> none  [the longest x1 14.4 us: body(): lax.all_to_all(inputs, 'ctx', split_axis=1, concat_axis=2, tiled=True)]
    all_to_all x3 -> x0, starting transfers between devices: 19 us -> none  [the longest x1 10.4 us: body(): lax.all_to_all(inputs, 'ctx', split_axis=1, concat_axis=2, tiled=True)]
    dot_general x8 -> x0, matrix products: 14.8 us -> none  [the longest x1 6.96 us: project(): jnp.dot(columns, lax.all_gather(out_cotangent, 'tp', axis=0, tiled=True),...]
    all_to_all x1 -> x0, blocking collectives: 12.1 us -> none  [body(): lax.all_to_all(gated_local, 'ctx', split_axis=1, concat_axis=0, tiled=True)]
  transfers between devices with their start and end apart: 6 -> 0, of which waited for: 4 -> 0; matrix products, arithmetic and copies ran while one was open for 8% -> 0% of each run, Pallas kernels for 0% -> 0%
where the time goes in v1:
time: 115 us
  Pallas kernels  107 us (93%)
  local copies, waits for them, and re-layouts  7.54 us (7%)
    pallas_call x1, Pallas kernels, body(): pl.pallas_call(kernel, out_shape=(jax.ShapeDtypeStruct((512, 128), BF), j...  107 us
    unnamed x15, local copies, waits for them, and re-layouts  6.96 us

profile of v1, /device:TPU:1, one launch (start us, length us, event | category | flops | bytes accessed | tf_op | source)
XLA Modules:
  0.0 114.9 jit_solution(7288658342363059277)
XLA Ops:
  0.6 0.0 copy-start
  0.6 1.0 copy-done
  1.6 0.0 copy-start.1
  1.6 0.9 copy-done.1
  2.6 0.0 copy-start.2
  2.6 0.9 copy-done.2
  3.5 0.0 copy-start.3
  3.5 0.7 copy-done.3
  4.2 0.0 copy-start.4
  4.2 0.7 copy-done.4
  4.9 0.0 copy-start.5
  4.9 0.7 copy-done.5
  5.6 106.7 %shard_map.93 = (bf16[512,128]{1,0:T(8,128)(2,1)S(1)}, bf16[3,512,128]{2,1,0:T(8,128)(2,1)S(1)}, f32[32,128]{1,0:T(8,128)S(1)}, f32[8,128]{1,0:T(8,128)S(1)}) custom-call(bf16[3,512,128]{2,1,0:T(8,128)(2,1)S(1)} %copy-done, f32[3,3,512]{2,1,0:T(4,128)S(1)} %copy-done.3, bf16[32,128]{1,0:T(8,128)(2,1)S(1)} %copy-done.4, f32[1,512]{1,0:T(1,128)S(1)} %bitcast.3, ...), custom_call_target="tpu_custom_call" | custom-call | flops 2600000000 | bytes 4000000 | tf_op jit(solution)/shard_map/pallas_call | solution.py:488
  112.3 0.6 slice_bitcast_fusion
  112.9 0.7 copy.13
  113.6 0.7 copy.14
  114.3 0.6 copy.15
Async XLA Ops:
  0.6 1.0 copy-start
  1.6 0.9 copy-start.1
  2.6 0.9 copy-start.2
  3.5 0.7 copy-start.3
  4.2 0.7 copy-start.4
  4.9 0.7 copy-start.5

commit v2 on v1

v2 whole, which is shorter than its diff:
```python
import jax
import jax.numpy as jnp
from jax import lax
from jax.experimental import pallas as pl
from jax.experimental.pallas import tpu as pltpu
from jax.sharding import PartitionSpec as P

MESH = pl.DeviceIdType.MESH
BF = jnp.bfloat16
F32 = jnp.float32
N_SEND = 128
N_RECV = 128


def nt_dot(a, b):
    return lax.dot_general(a, b, (((1,), (1,)), ((), ())), preferred_element_type=F32)


def tn_dot(a, b):
    return lax.dot_general(a, b, (((0,), (0,)), ((), ())), preferred_element_type=F32)


def nn_dot(a, b):
    return jnp.dot(a, b, preferred_element_type=F32)


def kernel(
    inp_hbm, taps_hbm, filt_hbm, skip_hbm, w_hbm, cot_hbm,
    out, ginp, gfilt, gskip,
    inp, taps, filt, skip, wall, call, toep, coef, tail_out, tail_in, tail_cols, qf, kf, vf, prod, prev, resp, gated_t,
    acc, acc_in, part, gout, gnext, gtail_out, gtail_in, gtail_cols,
    y_half, y_full, y_stage, z_half, z_full, z_stage, z_own, fin, fin_out, fin_in,
    pay, pay_in, local_sem, ssem, rsem, wz_sem,
):
    ctx, tp = lax.axis_index("ctx"), lax.axis_index("tp")
    x, zl, core = ctx // 8, (ctx // 2) % 4, ctx % 2
    zh, y = tp // 4, tp % 4
    own = x * 4 + zl

    local = [
        pltpu.make_async_copy(w_hbm, wall.at[own], local_sem.at[0]),
        pltpu.make_async_copy(inp_hbm, inp, local_sem.at[1]),
        pltpu.make_async_copy(taps_hbm, taps, local_sem.at[2]),
        pltpu.make_async_copy(skip_hbm, skip, local_sem.at[3]),
        pltpu.make_async_copy(filt_hbm, filt, local_sem.at[4]),
        pltpu.make_async_copy(cot_hbm.at[pl.ds(pl.multiple_of(core * 256, 256), 256), :], call.at[tp, core], local_sem.at[5]),
    ]
    for copy in local:
        copy.start()

    def at_ctx(x_, zl_, core_):
        return ((x_ * 4 + zl_) * 2 + core_, tp)

    def at_tp(zh_, y_):
        return (ctx, zh_ * 4 + y_)

    def plus(v, d):
        return (v + d) % 4

    x_right, x_left, x_far = at_ctx(plus(x, 1), zl, core), at_ctx(plus(x, 3), zl, core), at_ctx(plus(x, 2), zl, core)
    l_up, l_down, l_far = at_ctx(x, plus(zl, 1), core), at_ctx(x, plus(zl, 3), core), at_ctx(x, plus(zl, 2), core)
    sibling = at_ctx(x, zl, 1 - core)
    later, earlier = ((ctx + 1) % 32, tp), ((ctx + 31) % 32, tp)
    h_right, h_left = at_tp(plus(zh, 1), y), at_tp(plus(zh, 3), y)
    y_right, y_left = at_tp(zh, plus(y, 1)), at_tp(zh, plus(y, 3))

    upper = zl // 2
    inner = zl + upper * (3 - 2 * zl)
    step_dir = 1 - 2 * upper
    z_in = at_ctx(x, zl + step_dir, core)
    z_out = at_ctx(x, (zl - step_dir + 4) % 4, core)

    def unmirror(v):
        return v + upper * (3 - 2 * v)

    line = [zl, unmirror(1 - inner), unmirror(2), unmirror(3)]

    partners = [x_right, x_left, x_far, l_up, l_down, l_far, sibling, later, earlier, h_right, h_left, y_right, y_left]
    barrier = pltpu.get_barrier_semaphore()
    for who in partners:
        pl.semaphore_signal(barrier, inc=1, device_id=who, device_id_type=MESH)

    count = {"s": 0, "r": 0}
    sends = []

    def new_recv():
        count["r"] += 1
        return rsem.at[count["r"] - 1]

    def new_send():
        count["s"] += 1
        return ssem.at[count["s"] - 1]

    def send(src, dst, sem, who, when=None):
        copy = pltpu.make_async_remote_copy(src, dst, new_send(), sem, device_id=who, device_id_type=MESH)
        if when is None:
            copy.start()
        else:
            pl.when(when)(lambda: copy.start())
        sends.append((copy, when))

    def arrived(dst, sem):
        pltpu.make_async_remote_copy(dst, dst, ssem.at[0], sem, device_id=sibling, device_id_type=MESH).wait_recv()

    local[1].wait()
    for a in range(3):
        turned = inp[a].astype(F32).T
        tail_out[2 * a:2 * a + 2, :] = turned[126:128, :]
    tail_out[6:8, :] = jnp.zeros((2, 512), F32)
    for copy in (local[2], local[3], local[4], local[5], local[0]):
        copy.wait()
    pl.semaphore_wait(barrier, len(partners))

    x_sems = [[new_recv() for _ in range(4)] for _ in range(4)]
    lo, hi = pl.ds(0, 256), pl.ds(256, 256)

    def w_start(s):
        n = x * 4 + line[s]
        block = wall.at[n]
        if s > 0:
            arrived(block, wz_sem.at[line[s]])
        if s == 0:
            send(block, block, wz_sem.at[line[s]], z_in)
            send(block, block, wz_sem.at[line[s]], z_out, inner == 1)
        elif s == 1:
            send(block, block, wz_sem.at[line[s]], z_in, inner == 1)
        else:
            send(block, block, wz_sem.at[line[s]], z_out, inner == 1)
        send(block, block, x_sems[s][0], x_right)
        send(block, block, x_sems[s][1], x_left)

    def w_near(s):
        n = plus(x, 3) * 4 + line[s]
        arrived(wall.at[n], x_sems[s][0])
        half = wall.at[n, lo, :]
        send(half, half, x_sems[s][2], x_right)
        n = plus(x, 1) * 4 + line[s]
        arrived(wall.at[n], x_sems[s][1])
        half = wall.at[n, hi, :]
        send(half, half, x_sems[s][3], x_left)

    def w_far(s):
        n = plus(x, 2) * 4 + line[s]
        arrived(wall.at[n, lo, :], x_sems[s][2])
        arrived(wall.at[n, hi, :], x_sems[s][3])

    r_cot = new_recv()
    c_zn = [[new_recv() for _ in range(2)] for _ in range(2)]
    c_zf = [new_recv() for _ in range(2)]
    c_ys = [[new_recv() for _ in range(4)] for _ in range(4)]

    def c_zsend(p):
        block = call.at[tp, p]
        send(block, block, c_zn[p][0], h_right)
        send(block, block, c_zn[p][1], h_left)

    def c_zforward(p):
        n = plus(zh, 3 - 2 * p) * 4 + y
        block = call.at[n, p]
        arrived(block, c_zn[p][p])
        send(block, block, c_zf[p], (h_right, h_left)[p])

    def c_znear(d):
        n = plus(zh, d) * 4 + y
        way = (3 - d) // 2
        arrived(call.at[n, 1 - way], c_zn[1 - way][way])

    def c_zfar():
        n = plus(zh, 2) * 4 + y
        arrived(call.at[n, 0], c_zf[0])
        arrived(call.at[n, 1], c_zf[1])

    def c_ysend(d):
        block = call.at[plus(zh, d) * 4 + y]
        send(block, block, c_ys[d][0], y_right)
        send(block, block, c_ys[d][1], y_left)

    def c_ynear(d):
        n = plus(zh, d) * 4 + plus(y, 3)
        arrived(call.at[n], c_ys[d][0])
        send(call.at[n, 0], call.at[n, 0], c_ys[d][2], y_right)
        n = plus(zh, d) * 4 + plus(y, 1)
        arrived(call.at[n], c_ys[d][1])
        send(call.at[n, 1], call.at[n, 1], c_ys[d][3], y_left)

    def c_yfar(d):
        n = plus(zh, d) * 4 + plus(y, 2)
        arrived(call.at[n, 0], c_ys[d][2])
        arrived(call.at[n, 1], c_ys[d][3])

    def build(g16, carry):
        rows16 = filt[pl.ds(pl.multiple_of(g16 * 16, 16), 16), :].astype(F32)
        for r in range(16):
            row = jnp.concatenate([rows16[r:r + 1, :], jnp.zeros((1, 128), F32)], axis=1)
            wide = jnp.broadcast_to(row, (128, 256))
            toep[g16 * 16 + r] = pltpu.roll(wide, 0, 1, stride=1, stride_axis=0).astype(BF)
        return carry

    lane = lax.broadcasted_iota(jnp.int32, (64, 128), 1)

    def featurize(i, carry):
        rows = pl.ds(pl.multiple_of(i * 64, 64), 64)
        co = coef[rows, :]
        tl = tail_cols[rows, :]
        feats = []
        for a in range(3):
            v = inp[a, rows, :].astype(F32)
            t126, t127 = tl[:, 2 * a:2 * a + 1], tl[:, 2 * a + 1:2 * a + 2]
            v1 = jnp.where(lane == 0, t127, pltpu.roll(v, 1, 1))
            v2 = jnp.where(lane == 0, t126, jnp.where(lane == 1, t127, pltpu.roll(v, 2, 1)))
            feats.append(co[:, 3 * a:3 * a + 1] * v + co[:, 3 * a + 1:3 * a + 2] * v1 + co[:, 3 * a + 2:3 * a + 3] * v2)
        qf[rows, :] = feats[0]
        kf[rows, :] = feats[1]
        vf[rows, :] = feats[2]
        prod[rows, :] = (feats[1] * feats[2]).astype(BF)
        return carry

    def convolve(i, carry):
        pieces = []
        for j in range(8):
            rows = pl.ds(pl.multiple_of(i * 128 + j * 16, 16), 16)
            g = i * 8 + j
            cur = prod[rows, :]
            r = nn_dot(cur, toep[g, :, 0:128]) + nn_dot(prev[rows, :], toep[g, :, 128:256])
            r = r + coef[rows, 9:10] * cur.astype(F32)
            resp[rows, :] = r
            pieces.append(qf[rows, :] * r)
        columns = pl.ds(pl.multiple_of(i * 128, 128), 128)
        gated_t[core, :, columns] = jnp.concatenate(pieces, axis=0).T.astype(BF)
        return carry

    def forward(dx, steps):
        tokens = jnp.concatenate([gated_t[0], gated_t[1]], axis=0)
        for s in steps:
            n = plus(x, dx) * 4 + line[s]
            r = nn_dot(tokens, wall[n]).astype(BF)
            part[n, 0] = r[0:128, :]
            part[n, 1] = r[128:256, :]

    def backward(dx, steps, first=False):
        def one(r, carry):
            rows = pl.ds(pl.multiple_of(r * 128, 128), 128)
            total = None if first else jnp.concatenate([acc[0, rows, :], acc[1, rows, :]], axis=1)
            for s in steps:
                n = plus(x, dx) * 4 + line[s]
                term = nn_dot(wall[n, rows, :], jnp.concatenate([call[n, 0], call[n, 1]], axis=1))
                total = term if total is None else total + term
            acc[0, rows, :] = total[:, 0:128]
            acc[1, rows, :] = total[:, 128:256]
            return carry

        lax.fori_loop(0, 4, one, 0)

    yh = [[new_recv() for _ in range(2)] for _ in range(4)]
    yf = [[new_recv() for _ in range(2)] for _ in range(4)]
    zhs = [new_recv() for _ in range(2)]
    zfs = [new_recv() for _ in range(2)]
    zss = [new_send() for _ in range(4)]

    def y_begin(dx):
        far = plus(zh, dx) * 4 + plus(y, 2)
        send(part.at[far, 0], y_half.at[dx, 0], yh[dx][0], y_right)
        send(part.at[far, 1], y_half.at[dx, 1], yh[dx][1], y_left)

    def y_merge(dx):
        group = plus(zh, dx) * 4
        for way, who in ((0, y_right), (1, y_left)):
            n = group + plus(y, 1 + 2 * way)
            arrived(y_half.at[dx, way], yh[dx][way])
            y_stage[dx, way, way] = (part[n, way].astype(F32) + y_half[dx, way].astype(F32)).astype(BF)
            y_stage[dx, way, 1 - way] = part[n, 1 - way]
            send(y_stage.at[dx, way], y_full.at[dx, way], yf[dx][way], who)

    z_far = [
        pltpu.make_async_remote_copy(z_stage.at[0, i], z_half.at[i], zss[i], zhs[i], device_id=who, device_id_type=MESH)
        for i, who in enumerate((h_right, h_left))
    ]
    z_near = [
        pltpu.make_async_remote_copy(z_stage.at[1 + i], z_full.at[i], zss[2 + i], zfs[i], device_id=who, device_id_type=MESH)
        for i, who in enumerate((h_right, h_left))
    ]

    def y_sum(d):
        arrived(y_full.at[d, 0], yf[d][0])
        arrived(y_full.at[d, 1], yf[d][1])
        n = plus(zh, d) * 4 + y
        return [
            part[n, i].astype(F32) + y_full[d, 0, i].astype(F32) + y_full[d, 1, i].astype(F32) for i in range(2)
        ]

    def z_first():
        sums = y_sum(2)
        for i in range(2):
            z_stage[0, i] = sums[i].astype(BF)
            z_far[i].start()

    def z_second(way):
        sums = y_sum(1 + 2 * way)
        z_stage[1 + way, 1 - way] = sums[1 - way].astype(BF)
        arrived(z_half.at[way], zhs[way])
        z_stage[1 + way, way] = (sums[way] + z_half[way].astype(F32)).astype(BF)
        z_near[way].start()

    def z_third():
        sums = y_sum(0)
        for i in range(2):
            z_own[i] = sums[i]

    turn = (
        lax.broadcasted_iota(jnp.int32, (128, 128), 0) + lax.broadcasted_iota(jnp.int32, (128, 128), 1) == 127
    ).astype(F32).astype(BF)

    def at_response(i, carry):
        rows = pl.ds(pl.multiple_of(i * 64, 64), 64)
        gg = (acc[core, rows, :] + acc_in[rows, :]).astype(BF).astype(F32)
        gout[rows, :] = (gg * qf[rows, :]).astype(BF)
        qf[rows, :] = gg * resp[rows, :]
        return carry

    def grad_product(i, carry):
        for j in range(8):
            rows = pl.ds(pl.multiple_of(i * 128 + j * 16, 16), 16)
            g = i * 8 + j
            gr = gout[rows, :]
            r = nt_dot(gr, toep[g, :, 0:128]) + nt_dot(gnext[rows, :], toep[g, :, 128:256])
            r = r + coef[rows, 9:10] * gr.astype(F32)
            k = kf[rows, :]
            kf[rows, :] = r * vf[rows, :]
            vf[rows, :] = r * k
        return carry

    def correlate(i, carry):
        base = pl.multiple_of(i * 128, 128)
        cur = nn_dot(prod[pl.ds(base, 128), :], turn).astype(BF)
        back = nn_dot(prev[pl.ds(base, 128), :], turn).astype(BF)
        sums = []
        for j in range(8):
            gr = gout[pl.ds(pl.multiple_of(i * 128 + j * 16, 16), 16), :]
            one = tn_dot(cur[16 * j:16 * (j + 1), :], gr)
            two = tn_dot(back[16 * j:16 * (j + 1), :], gr)
            both = pltpu.roll(jnp.concatenate([one, two], axis=1), 129, 1, stride=1, stride_axis=0)
            sums.append(jnp.sum(both[:, 0:128], axis=0, keepdims=True))
        pay[0, pl.ds(pl.multiple_of(i * 8, 8), 8), :] = jnp.concatenate(sums, axis=0)
        return carry

    def exchange(stage, targets):
        sems = [new_recv() for _ in targets]
        for i, who in enumerate(targets):
            send(pay.at[stage], pay_in.at[stage, i], sems[i], who)
        return sems

    def collect(stage, sems):
        total = pay[stage]
        for i, sem in enumerate(sems):
            arrived(pay_in.at[stage, i], sem)
            total = total + pay_in[stage, i]
        return total

    def short_back(i, carry):
        rows = pl.ds(pl.multiple_of(i * 64, 64), 64)
        co = coef[rows, :]
        tl = gtail_cols[rows, :]
        for a, ref in enumerate((qf, kf, vf)):
            v = ref[rows, :]
            t0, t1 = tl[:, 2 * a:2 * a + 1], tl[:, 2 * a + 1:2 * a + 2]
            v1 = jnp.where(lane == 127, t0, pltpu.roll(v, 127, 1))
            v2 = jnp.where(lane == 126, t0, jnp.where(lane == 127, t1, pltpu.roll(v, 126, 1)))
            r = co[:, 3 * a:3 * a + 1] * v + co[:, 3 * a + 1:3 * a + 2] * v1 + co[:, 3 * a + 2:3 * a + 3] * v2
            ginp[a, rows, :] = r.astype(BF)
        return carry

    w_start(0)
    r_tail = new_recv()
    send(tail_out, tail_in, r_tail, later)
    theirs = pl.ds(pl.multiple_of((1 - core) * 256, 256), 256)
    send(cot_hbm.at[theirs, :], call.at[tp, core], r_cot, sibling)

    table = jnp.concatenate([taps[0], taps[1], taps[2], skip[...], jnp.zeros((6, 512), F32)], axis=0)
    coef[...] = table.T
    arrived(tail_in, r_tail)
    tail_cols[...] = jnp.where(ctx == 0, 0.0, tail_in[...]).T
    lax.fori_loop(0, 8, featurize, 0)
    r_prod = new_recv()
    send(prod, prev, r_prod, later)
    arrived(call.at[tp, 1 - core], r_cot)
    c_zsend(0)
    c_zsend(1)
    c_ysend(0)
    lax.fori_loop(0, 2, build, 0)

    w_start(1)
    w_near(0)
    arrived(prev, r_prod)

    @pl.when(ctx == 0)
    def _():
        prev[...] = jnp.zeros((512, 128), BF)

    lax.fori_loop(0, 4, convolve, 0)
    r_gated = new_recv()
    send(gated_t.at[core], gated_t.at[core], r_gated, sibling)
    w_start(2)
    c_ynear(0)
    w_near(1)
    c_zforward(0)
    c_zforward(1)
    c_znear(3)
    c_znear(1)
    c_ysend(3)
    c_ysend(1)
    arrived(gated_t.at[1 - core], r_gated)
    w_start(3)
    w_far(0)
    forward(0, (0, 1, 2, 3))
    for d in (3, 1, 2):
        forward(d, (0,))
    c_zfar()
    c_ysend(2)
    w_near(2)
    c_yfar(0)
    c_ynear(3)
    c_ynear(1)
    w_far(1)
    for d in (3, 1, 2):
        forward(d, (1,))
    w_near(3)
    c_ynear(2)
    c_yfar(3)
    c_yfar(1)
    c_yfar(2)
    w_far(2)
    forward(3, (2, 3))
    forward(1, (2, 3))
    forward(2, (2,))
    backward(0, (0, 1, 2, 3), True)
    backward(3, (0, 1, 2, 3))
    backward(1, (0, 1, 2, 3))
    w_far(3)
    forward(2, (3,))
    for d in (2, 1, 3, 0):
        y_begin(d)
    backward(2, (0, 1, 2, 3))
    r_acc = new_recv()
    send(acc.at[1 - core], acc_in, r_acc, sibling)
    arrived(acc_in, r_acc)
    lax.fori_loop(0, 8, at_response, 0)
    r_gout = new_recv()
    send(gout, gnext, r_gout, earlier)
    for d in (2, 1, 3, 0):
        y_merge(d)
    arrived(gnext, r_gout)

    @pl.when(ctx == 31)
    def _():
        gnext[...] = jnp.zeros((512, 128), BF)

    lax.fori_loop(0, 4, grad_product, 0)
    for a, ref in enumerate((qf, kf, vf)):
        gtail_out[2 * a:2 * a + 2, :] = ref[:, 0:128].T[0:2, :]
    gtail_out[6:8, :] = jnp.zeros((2, 512), F32)
    r_gtail = new_recv()
    send(gtail_out, gtail_in, r_gtail, earlier)
    z_first()
    lax.fori_loop(0, 4, correlate, 0)
    for i in range(4):
        both = gout[128 * i:128 * (i + 1), :].astype(F32) * prod[128 * i:128 * (i + 1), :].astype(F32)
        pay[0, 32 + i:33 + i, :] = jnp.sum(both.T, axis=0, keepdims=True)
    pay[0, 36:40, :] = jnp.zeros((4, 128), F32)
    px = exchange(0, [x_right, x_left, x_far])
    z_second(0)
    z_second(1)
    z_third()
    pay[1] = collect(0, px)
    pz = exchange(1, [l_up, l_down, l_far])

    arrived(gtail_in, r_gtail)
    gtail_cols[...] = jnp.where(ctx == 31, 0.0, gtail_in[...]).T
    lax.fori_loop(0, 8, short_back, 0)
    pay[2] = collect(1, pz)
    pc = exchange(2, [sibling])

    arrived(z_full.at[0], zfs[0])
    arrived(z_full.at[1], zfs[1])
    fin[...] = z_own[...] + z_full[0].astype(F32) + z_full[1].astype(F32)
    fin_out[...] = fin[1 - core].astype(BF)
    r_fin = new_recv()
    send(fin_out, fin_in, r_fin, sibling)
    out[pl.ds(pl.multiple_of(core * 256, 256), 256), :] = fin[core].T.astype(BF)
    total = collect(2, pc)
    gfilt[...] = total[0:32, :]
    gskip[...] = total[32:40, :]
    arrived(fin_in, r_fin)
    out[theirs, :] = fin_in[...].astype(F32).T.astype(BF)

    for copy, when in sends:
        if when is None:
            copy.wait_send()
        else:
            pl.when(when)(lambda copy=copy: copy.wait_send())
    for copy in z_far + z_near:
        copy.wait_send()
    assert count["s"] <= N_SEND and count["r"] <= N_RECV


def body(inputs, short_filters, explicit_filter, skip_gain, out_weight, out_cotangent):
    vmem = pl.BlockSpec(memory_space=pltpu.VMEM)
    hbm = pl.BlockSpec(memory_space=pltpu.HBM)
    out, ginp, gfilt, gskip = pl.pallas_call(
        kernel,
        out_shape=(
            jax.ShapeDtypeStruct((512, 128), BF),
            jax.ShapeDtypeStruct((3, 512, 128), BF),
            jax.ShapeDtypeStruct((32, 128), F32),
            jax.ShapeDtypeStruct((8, 128), F32),
        ),
        in_specs=[hbm] * 6,
        out_specs=(vmem, vmem, vmem, vmem),
        scratch_shapes=[
            pltpu.VMEM((3, 512, 128), BF),
            pltpu.VMEM((3, 3, 512), F32),
            pltpu.VMEM((32, 128), BF),
            pltpu.VMEM((1, 512), F32),
            pltpu.VMEM((16, 512, 256), BF),
            pltpu.VMEM((16, 2, 256, 128), BF),
            pltpu.VMEM((32, 128, 256), BF),
            pltpu.VMEM((512, 16), F32),
            pltpu.VMEM((8, 512), F32),
            pltpu.VMEM((8, 512), F32),
            pltpu.VMEM((512, 8), F32),
            pltpu.VMEM((512, 128), F32),
            pltpu.VMEM((512, 128), F32),
            pltpu.VMEM((512, 128), F32),
            pltpu.VMEM((512, 128), BF),
            pltpu.VMEM((512, 128), BF),
            pltpu.VMEM((512, 128), F32),
            pltpu.VMEM((2, 128, 512), BF),
            pltpu.VMEM((2, 512, 128), F32),
            pltpu.VMEM((512, 128), F32),
            pltpu.VMEM((16, 2, 128, 256), BF),
            pltpu.VMEM((512, 128), BF),
            pltpu.VMEM((512, 128), BF),
            pltpu.VMEM((8, 512), F32),
            pltpu.VMEM((8, 512), F32),
            pltpu.VMEM((512, 8), F32),
            pltpu.VMEM((4, 2, 128, 256), BF),
            pltpu.VMEM((4, 2, 2, 128, 256), BF),
            pltpu.VMEM((4, 2, 2, 128, 256), BF),
            pltpu.VMEM((2, 128, 256), BF),
            pltpu.VMEM((2, 2, 128, 256), BF),
            pltpu.VMEM((3, 2, 128, 256), BF),
            pltpu.VMEM((2, 128, 256), F32),
            pltpu.VMEM((2, 128, 256), F32),
            pltpu.VMEM((128, 256), BF),
            pltpu.VMEM((128, 256), BF),
            pltpu.VMEM((3, 40, 128), F32),
            pltpu.VMEM((3, 3, 40, 128), F32),
            pltpu.SemaphoreType.DMA((6,)),
            pltpu.SemaphoreType.DMA((N_SEND,)),
            pltpu.SemaphoreType.DMA((N_RECV,)),
            pltpu.SemaphoreType.DMA((4,)),
        ],
        compiler_params=pltpu.CompilerParams(
            collective_id=0, has_side_effects=True, vmem_limit_bytes=60 * 1024 * 1024
        ),
        cost_estimate=pl.CostEstimate(flops=2600000000, bytes_accessed=4000000, transcendentals=0),
    )(inputs, short_filters, explicit_filter, skip_gain.reshape(1, 512), out_weight, out_cotangent)
    return (out, ginp, gfilt, gskip[0:4].reshape(512))


def solution(mesh):
    placed = (
        P(None, "tp", "ctx"),
        P(None, None, "tp"),
        P("tp", None),
        P("tp"),
        P("tp", "ctx"),
        P("tp", "ctx"),
    )
    return jax.shard_map(
        body,
        mesh=mesh,
        in_specs=placed,
        out_specs=(P("tp", "ctx"), P(None, "tp", "ctx"), P("tp", None), P("tp")),
        check_vma=False,
    )
```

time: 115 us -> 107 us (0.930)
  Pallas kernels: 107 us -> 101 us
  local copies, waits for them, and re-layouts: 7.54 us -> 5.21 us
    pallas_call x1, Pallas kernels: 107 us -> 101 us  [body(): pl.pallas_call(kernel, out_shape=(jax.ShapeDtypeStruct((512, 128), BF), j...]
    unnamed x15 -> x7, local copies, waits for them, and re-layouts: 6.96 us -> 4.63 us
where the time goes in v2:
time: 107 us
  Pallas kernels  101 us (94%)
  local copies, waits for them, and re-layouts  5.21 us (5%)
    pallas_call x1, Pallas kernels, body(): pl.pallas_call(kernel, out_shape=(jax.ShapeDtypeStruct((512, 128), BF), j...  101 us
    unnamed x7, local copies, waits for them, and re-layouts  4.63 us

profile of v2, /device:TPU:1, one launch (start us, length us, event | category | flops | bytes accessed | tf_op | source)
XLA Modules:
  0.0 107.1 jit_solution(14982546372119452839)
XLA Ops:
  0.6 101.2 %shard_map.93 = (bf16[512,128]{1,0:T(8,128)(2,1)}, bf16[3,512,128]{2,1,0:T(8,128)(2,1)}, f32[32,128]{1,0:T(8,128)}, f32[8,128]{1,0:T(8,128)}) custom-call(bf16[3,512,128]{2,1,0:T(8,128)(2,1)} %inp_hbm.1, f32[3,3,512]{2,1,0:T(4,128)} %taps_hbm.1, bf16[32,128]{1,0:T(8,128)(2,1)} %filt_hbm.1, f32[1,512]{1,0:T(1,128)} %bitcast.3, bf16[512,256]{1,0:T(8,128)(2,1)} %w_hbm.1, ...), custom_call_target="tpu_custom_call" | custom-call | flops 2600000000 | bytes 4000000 | tf_op jit(solution)/shard_map/pallas_call | solution.py:508
  101.9 0.0 copy-start.1
  101.9 0.7 copy-done.1
  102.5 0.6 slice_bitcast_fusion
  103.1 1.6 %copy.13 = bf16[512,128]{1,0:T(8,128)(2,1)} copy(bf16[512,128]{1,0:T(8,128)(2,1)} %get-tuple-element.16) | data formatting | bytes 262144
  104.7 0.0 copy-start
  104.7 1.8 %copy.14 = bf16[3,512,128]{2,1,0:T(8,128)(2,1)} copy(bf16[3,512,128]{2,1,0:T(8,128)(2,1)} %get-tuple-element.17) | data formatting | bytes 786432
  106.5 0.0 copy-done
  106.5 0.6 copy.15
Async XLA Ops:
  101.9 0.7 copy-start.1
  104.7 1.8 %copy-start = (f32[32,128]{1,0:T(8,128)S(1)}, f32[32,128]{1,0:T(8,128)}, u32[]{:S(2)}) copy-start(f32[32,128]{1,0:T(8,128)} %get-tuple-element.18) | copy-start | bytes 49156

commit v3 on v2

--- a/solution.py
+++ b/solution.py
@@ -29,8 +29,8 @@
     out, ginp, gfilt, gskip,
     inp, taps, filt, skip, wall, call, toep, coef, tail_out, tail_in, tail_cols, qf, kf, vf, prod, prev, resp, gated_t,
     acc, acc_in, part, gout, gnext, gtail_out, gtail_in, gtail_cols,
-    y_half, y_full, y_stage, z_half, z_full, z_stage, z_own, fin, fin_out, fin_in,
-    pay, pay_in, local_sem, ssem, rsem, wz_sem,
+    y_half, y_full, y_stage, z_half, z_full, z_stage, z_own, z_mid, fin, fin_out, fin_in,
+    pay, pay_in, local_sem, ssem, rsem, wz_sem, y_sem,
 ):
     ctx, tp = lax.axis_index("ctx"), lax.axis_index("tp")
     x, zl, core = ctx // 8, (ctx // 2) % 4, ctx % 2
@@ -251,41 +251,43 @@
 
         lax.fori_loop(0, 4, one, 0)
 
-    yh = [[new_recv() for _ in range(2)] for _ in range(4)]
-    yf = [[new_recv() for _ in range(2)] for _ in range(4)]
     zhs = [new_recv() for _ in range(2)]
-    zfs = [new_recv() for _ in range(2)]
-    zss = [new_send() for _ in range(4)]
+    zfs = [[new_recv() for _ in range(2)] for _ in range(2)]
+    zss = [new_send() for _ in range(6)]
 
     def y_begin(dx):
-        far = plus(zh, dx) * 4 + plus(y, 2)
-        send(part.at[far, 0], y_half.at[dx, 0], yh[dx][0], y_right)
-        send(part.at[far, 1], y_half.at[dx, 1], yh[dx][1], y_left)
+        group = plus(x, dx)
+        far = group * 4 + plus(y, 2)
+        send(part.at[far, 0], y_half.at[group, 0], y_sem.at[group * 4], y_right)
+        send(part.at[far, 1], y_half.at[group, 1], y_sem.at[group * 4 + 1], y_left)
 
     def y_merge(dx):
-        group = plus(zh, dx) * 4
+        group = plus(x, dx)
         for way, who in ((0, y_right), (1, y_left)):
-            n = group + plus(y, 1 + 2 * way)
-            arrived(y_half.at[dx, way], yh[dx][way])
-            y_stage[dx, way, way] = (part[n, way].astype(F32) + y_half[dx, way].astype(F32)).astype(BF)
+            n = group * 4 + plus(y, 1 + 2 * way)
+            arrived(y_half.at[group, way], y_sem.at[group * 4 + way])
+            y_stage[dx, way, way] = (part[n, way].astype(F32) + y_half[group, way].astype(F32)).astype(BF)
             y_stage[dx, way, 1 - way] = part[n, 1 - way]
-            send(y_stage.at[dx, way], y_full.at[dx, way], yf[dx][way], who)
+            send(y_stage.at[dx, way], y_full.at[group, way], y_sem.at[group * 4 + 2 + way], who)
 
     z_far = [
         pltpu.make_async_remote_copy(z_stage.at[0, i], z_half.at[i], zss[i], zhs[i], device_id=who, device_id_type=MESH)
         for i, who in enumerate((h_right, h_left))
     ]
     z_near = [
-        pltpu.make_async_remote_copy(z_stage.at[1 + i], z_full.at[i], zss[2 + i], zfs[i], device_id=who, device_id_type=MESH)
-        for i, who in enumerate((h_right, h_left))
+        pltpu.make_async_remote_copy(
+            z_stage.at[1 + way, i], z_full.at[way, i], zss[2 + 2 * way + i], zfs[way][i], device_id=who, device_id_type=MESH
+        )
+        for way, who in enumerate((h_right, h_left)) for i in range(2)
     ]
 
     def y_sum(d):
-        arrived(y_full.at[d, 0], yf[d][0])
-        arrived(y_full.at[d, 1], yf[d][1])
-        n = plus(zh, d) * 4 + y
+        group = plus(zh, d)
+        arrived(y_full.at[group, 0], y_sem.at[group * 4 + 2])
+        arrived(y_full.at[group, 1], y_sem.at[group * 4 + 3])
         return [
-            part[n, i].astype(F32) + y_full[d, 0, i].astype(F32) + y_full[d, 1, i].astype(F32) for i in range(2)
+            part[group * 4 + y, i].astype(F32) + y_full[group, 0, i].astype(F32) + y_full[group, 1, i].astype(F32)
+            for i in range(2)
         ]
 
     def z_first():
@@ -294,12 +296,16 @@
             z_stage[0, i] = sums[i].astype(BF)
             z_far[i].start()
 
-    def z_second(way):
+    def z_open(way):
         sums = y_sum(1 + 2 * way)
         z_stage[1 + way, 1 - way] = sums[1 - way].astype(BF)
+        z_near[2 * way + 1 - way].start()
+        z_mid[way] = sums[way]
+
+    def z_second(way):
         arrived(z_half.at[way], zhs[way])
-        z_stage[1 + way, way] = (sums[way] + z_half[way].astype(F32)).astype(BF)
-        z_near[way].start()
+        z_stage[1 + way, way] = (z_mid[way] + z_half[way].astype(F32)).astype(BF)
+        z_near[3 * way].start()
 
     def z_third():
         sums = y_sum(0)
@@ -412,6 +418,7 @@
     w_start(3)
     w_far(0)
     forward(0, (0, 1, 2, 3))
+    y_begin(0)
     for d in (3, 1, 2):
         forward(d, (0,))
     c_zfar()
@@ -423,31 +430,43 @@
     w_far(1)
     for d in (3, 1, 2):
         forward(d, (1,))
+    y_merge(0)
     w_near(3)
+    forward(3, (2, 3))
+    y_begin(3)
+    forward(1, (2, 3))
+    y_begin(1)
+    w_far(2)
+    forward(2, (2,))
+    w_far(3)
+    forward(2, (3,))
+    y_begin(2)
     c_ynear(2)
+    y_merge(3)
+    y_merge(1)
+    y_merge(2)
     c_yfar(3)
     c_yfar(1)
     c_yfar(2)
-    w_far(2)
-    forward(3, (2, 3))
-    forward(1, (2, 3))
-    forward(2, (2,))
     backward(0, (0, 1, 2, 3), True)
     backward(3, (0, 1, 2, 3))
     backward(1, (0, 1, 2, 3))
-    w_far(3)
-    forward(2, (3,))
-    for d in (2, 1, 3, 0):
-        y_begin(d)
     backward(2, (0, 1, 2, 3))
     r_acc = new_recv()
     send(acc.at[1 - core], acc_in, r_acc, sibling)
+    z_first()
+    z_open(0)
+    z_open(1)
     arrived(acc_in, r_acc)
     lax.fori_loop(0, 8, at_response, 0)
     r_gout = new_recv()
     send(gout, gnext, r_gout, earlier)
-    for d in (2, 1, 3, 0):
-        y_merge(d)
+    lax.fori_loop(0, 4, correlate, 0)
+    for i in range(4):
+        both = gout[128 * i:128 * (i + 1), :].astype(F32) * prod[128 * i:128 * (i + 1), :].astype(F32)
+        pay[0, 32 + i:33 + i, :] = jnp.sum(both.T, axis=0, keepdims=True)
+    pay[0, 36:40, :] = jnp.zeros((4, 128), F32)
+    px = exchange(0, [x_right, x_left, x_far])
     arrived(gnext, r_gout)
 
     @pl.when(ctx == 31)
@@ -460,13 +479,6 @@
     gtail_out[6:8, :] = jnp.zeros((2, 512), F32)
     r_gtail = new_recv()
     send(gtail_out, gtail_in, r_gtail, earlier)
-    z_first()
-    lax.fori_loop(0, 4, correlate, 0)
-    for i in range(4):
-        both = gout[128 * i:128 * (i + 1), :].astype(F32) * prod[128 * i:128 * (i + 1), :].astype(F32)
-        pay[0, 32 + i:33 + i, :] = jnp.sum(both.T, axis=0, keepdims=True)
-    pay[0, 36:40, :] = jnp.zeros((4, 128), F32)
-    px = exchange(0, [x_right, x_left, x_far])
     z_second(0)
     z_second(1)
     z_third()
@@ -479,8 +491,9 @@
     pay[2] = collect(1, pz)
     pc = exchange(2, [sibling])
 
-    arrived(z_full.at[0], zfs[0])
-    arrived(z_full.at[1], zfs[1])
+    for way in range(2):
+        for i in range(2):
+            arrived(z_full.at[way, i], zfs[way][i])
     fin[...] = z_own[...] + z_full[0].astype(F32) + z_full[1].astype(F32)
     fin_out[...] = fin[1 - core].astype(BF)
     r_fin = new_recv()
@@ -550,6 +563,7 @@
             pltpu.VMEM((3, 2, 128, 256), BF),
             pltpu.VMEM((2, 128, 256), F32),
             pltpu.VMEM((2, 128, 256), F32),
+            pltpu.VMEM((2, 128, 256), F32),
             pltpu.VMEM((128, 256), BF),
             pltpu.VMEM((128, 256), BF),
             pltpu.VMEM((3, 40, 128), F32),
@@ -558,6 +572,7 @@
             pltpu.SemaphoreType.DMA((N_SEND,)),
             pltpu.SemaphoreType.DMA((N_RECV,)),
             pltpu.SemaphoreType.DMA((4,)),
+            pltpu.SemaphoreType.DMA((16,)),
         ],
         compiler_params=pltpu.CompilerParams(
             collective_id=0, has_side_effects=True, vmem_limit_bytes=60 * 1024 * 1024

time: 107 us -> 103 us (0.963)
  Pallas kernels: 101 us -> 96.9 us
    pallas_call x1, Pallas kernels: 101 us -> 96.9 us  [body(): pl.pallas_call(kernel, out_shape=(jax.ShapeDtypeStruct((512, 128), BF), j...]
where the time goes in v3:
time: 103 us
  Pallas kernels  96.9 us (94%)
  local copies, waits for them, and re-layouts  5.21 us (5%)
    pallas_call x1, Pallas kernels, body(): pl.pallas_call(kernel, out_shape=(jax.ShapeDtypeStruct((512, 128), BF), j...  96.9 us
    unnamed x7, local copies, waits for them, and re-layouts  4.63 us

profile of v3, /device:TPU:1, one launch (start us, length us, event | category | flops | bytes accessed | tf_op | source)
XLA Modules:
  0.0 102.8 jit_solution(11434454162726566436)
XLA Ops:
  0.6 96.9 %shard_map.93 = (bf16[512,128]{1,0:T(8,128)(2,1)}, bf16[3,512,128]{2,1,0:T(8,128)(2,1)}, f32[32,128]{1,0:T(8,128)}, f32[8,128]{1,0:T(8,128)}) custom-call(bf16[3,512,128]{2,1,0:T(8,128)(2,1)} %inp_hbm.1, f32[3,3,512]{2,1,0:T(4,128)} %taps_hbm.1, bf16[32,128]{1,0:T(8,128)(2,1)} %filt_hbm.1, f32[1,512]{1,0:T(1,128)} %bitcast.3, bf16[512,256]{1,0:T(8,128)(2,1)} %w_hbm.1, ...), custom_call_target="tpu_custom_call" | custom-call | flops 2600000000 | bytes 4000000 | tf_op jit(solution)/shard_map/pallas_call | solution.py:521
  97.5 0.0 copy-start.1
  97.5 0.7 copy-done.1
  98.2 0.6 slice_bitcast_fusion
  98.8 1.6 %copy.13 = bf16[512,128]{1,0:T(8,128)(2,1)} copy(bf16[512,128]{1,0:T(8,128)(2,1)} %get-tuple-element.16) | data formatting | bytes 262144
  100.4 0.0 copy-start
  100.4 1.8 %copy.14 = bf16[3,512,128]{2,1,0:T(8,128)(2,1)} copy(bf16[3,512,128]{2,1,0:T(8,128)(2,1)} %get-tuple-element.17) | data formatting | bytes 786432
  102.1 0.0 copy-done
  102.1 0.6 copy.15
Async XLA Ops:
  97.5 0.7 copy-start.1
  100.4 1.8 %copy-start = (f32[32,128]{1,0:T(8,128)S(1)}, f32[32,128]{1,0:T(8,128)}, u32[]{:S(2)}) copy-start(f32[32,128]{1,0:T(8,128)} %get-tuple-element.18) | copy-start | bytes 49156

commit v4 on v3

--- a/solution.py
+++ b/solution.py
@@ -26,7 +26,7 @@
 
 def kernel(
     inp_hbm, taps_hbm, filt_hbm, skip_hbm, w_hbm, cot_hbm,
-    out, ginp, gfilt, gskip,
+    out, ginp, gsums,
     inp, taps, filt, skip, wall, call, toep, coef, tail_out, tail_in, tail_cols, qf, kf, vf, prod, prev, resp, gated_t,
     acc, acc_in, part, gout, gnext, gtail_out, gtail_in, gtail_cols,
     y_half, y_full, y_stage, z_half, z_full, z_stage, z_own, z_mid, fin, fin_out, fin_in,
@@ -499,9 +499,7 @@
     r_fin = new_recv()
     send(fin_out, fin_in, r_fin, sibling)
     out[pl.ds(pl.multiple_of(core * 256, 256), 256), :] = fin[core].T.astype(BF)
-    total = collect(2, pc)
-    gfilt[...] = total[0:32, :]
-    gskip[...] = total[32:40, :]
+    gsums[...] = collect(2, pc)
     arrived(fin_in, r_fin)
     out[theirs, :] = fin_in[...].astype(F32).T.astype(BF)
 
@@ -518,16 +516,15 @@
 def body(inputs, short_filters, explicit_filter, skip_gain, out_weight, out_cotangent):
     vmem = pl.BlockSpec(memory_space=pltpu.VMEM)
     hbm = pl.BlockSpec(memory_space=pltpu.HBM)
-    out, ginp, gfilt, gskip = pl.pallas_call(
+    out, ginp, gsums = pl.pallas_call(
         kernel,
         out_shape=(
             jax.ShapeDtypeStruct((512, 128), BF),
             jax.ShapeDtypeStruct((3, 512, 128), BF),
-            jax.ShapeDtypeStruct((32, 128), F32),
-            jax.ShapeDtypeStruct((8, 128), F32),
+            jax.ShapeDtypeStruct((40, 128), F32),
         ),
         in_specs=[hbm] * 6,
-        out_specs=(vmem, vmem, vmem, vmem),
+        out_specs=(vmem, vmem, vmem),
         scratch_shapes=[
             pltpu.VMEM((3, 512, 128), BF),
             pltpu.VMEM((3, 3, 512), F32),
@@ -579,7 +576,7 @@
         ),
         cost_estimate=pl.CostEstimate(flops=2600000000, bytes_accessed=4000000, transcendentals=0),
     )(inputs, short_filters, explicit_filter, skip_gain.reshape(1, 512), out_weight, out_cotangent)
-    return (out, ginp, gfilt, gskip[0:4].reshape(512))
+    return (out, ginp, gsums[0:32], gsums[32:36].reshape(512))
 
 
 def solution(mesh):

time: 103 us -> 104 us (level)
    slice x0 -> x1, local copies, waits for them, and re-layouts: none -> 1.32 us  [body(): return (out, ginp, gsums[0:32], gsums[32:36].reshape(512))]
    unnamed x7 -> x2, local copies, waits for them, and re-layouts: 4.63 us -> 3.33 us
where the time goes in v4:
time: 104 us; the launch traced here: 103 us
  Pallas kernels  96.9 us (93%)
  local copies, waits for them, and re-layouts  5.92 us (6%)
    pallas_call x1, Pallas kernels, body(): pl.pallas_call(kernel, out_shape=(jax.ShapeDtypeStruct((512, 128), BF), j...  96.9 us
    unnamed x2, local copies, waits for them, and re-layouts  3.33 us

profile of v4, /device:TPU:1, one launch (start us, length us, event | category | flops | bytes accessed | tf_op | source)
XLA Modules:
  0.0 103.4 jit_solution(18168736697572123365)
XLA Ops:
  0.6 96.9 %shard_map.93 = (bf16[512,128]{1,0:T(8,128)(2,1)}, bf16[3,512,128]{2,1,0:T(8,128)(2,1)}, f32[40,128]{1,0:T(8,128)}) custom-call(bf16[3,512,128]{2,1,0:T(8,128)(2,1)} %inp_hbm.1, f32[3,3,512]{2,1,0:T(4,128)} %taps_hbm.1, bf16[32,128]{1,0:T(8,128)(2,1)} %filt_hbm.1, f32[1,512]{1,0:T(1,128)} %bitcast.3, bf16[512,256]{1,0:T(8,128)(2,1)} %w_hbm.1, ...), custom_call_target="tpu_custom_call" | custom-call | flops 2600000000 | bytes 4000000 | tf_op jit(solution)/shard_map/pallas_call | solution.py:519
  97.5 1.3 %slice_bitcast_fusion = f32[512]{0:T(512)} fusion(f32[40,128]{1,0:T(8,128)} %get-tuple-element.9), kind=kLoop, calls=%fused_computation | loop fusion | bytes 4096 | tf_op jit(solution)/shard_map/reshape | solution.py:579
  98.8 1.3 %slice.6 = f32[32,128]{1,0:T(8,128)} slice(f32[40,128]{1,0:T(8,128)} %get-tuple-element.9), slice={[0:32], [0:128]} | slice | bytes 32768 | tf_op jit(solution)/shard_map/slice | solution.py:579
  100.1 1.6 %copy.12 = bf16[512,128]{1,0:T(8,128)(2,1)} copy(bf16[512,128]{1,0:T(8,128)(2,1)} %get-tuple-element.14) | data formatting | bytes 262144
  101.7 1.8 %copy.13 = bf16[3,512,128]{2,1,0:T(8,128)(2,1)} copy(bf16[3,512,128]{2,1,0:T(8,128)(2,1)} %get-tuple-element.15) | data formatting | bytes 786432
